TPU v7x, 32 devices: a whole 2x2x4 slice. The times are simulated.
32 devices in a mesh: ctx: 16 (over z, y, x), ch: 2 (over core).
Axes of the slice: x: 2, y: 2, z: 4, core: 2. Of those that a mesh axis runs over, the one named last changes fastest.
Arguments:
- conv_input: bfloat16 [2048, 4096], P('ctx', 'ch'), may hold values from -6 to 6
- residues: float32 [4096, 16], P('ch'), may hold values from -4 to 4
- decay_rates: float32 [4096, 16], P('ch'), as said below
- skip_gain: float32 [4096], P('ch'), may hold values from -1 to 1
- query_rows: bfloat16 [2048, 4096], P('ctx', 'ch'), may hold values from -5 to 5
- key_rows: bfloat16 [2048, 4096], P('ctx', 'ch'), may hold values from -5 to 5
- value_rows: bfloat16 [2048, 4096], P('ctx', 'ch'), may hold values from -16 to 16
- norm_gain: float32 [4096], P('ch'), may hold values from 0.5 to 1.5
Outputs:
- conv_out: bfloat16 [2048, 4096], P('ctx', 'ch')
- attended: bfloat16 [2048, 4096], P('ctx', 'ch')
Inputs may be any that keep to these rules, and one draw needn't show every extreme that they name: `decay_rates`: decay rates lie between 0.5 / 2048 and 1 / 30.
All inputs are finite; a program needn't handle non-finite values.
Results may differ from a plain program's by a relative error of at most 0.019.
Values may be sent and summed in bfloat16 or wider, within the bound.
A program may use at most 64 MiB of HBM per device.

v0:
```python
import math

import jax
import jax.numpy as jnp
from jax import lax
from jax.sharding import PartitionSpec as P

HD = 128
WIDTH = 4096


HIGHEST = lax.Precision.HIGHEST


def partner_2(value, axis, apart):
    mask = 2**apart
    pairs = [(source, source ^ mask) for source in range(lax.axis_size(axis))]
    return lax.ppermute(value, axis, pairs)


def shifted(block, axis, distance):
    devices = range(lax.axis_size(axis))
    route = [(i - distance, i) for i in devices if i - distance in devices]
    return lax.ppermute(block, axis, route)


def rotate(real_part, imag_part, turn_angle):
    cosine = jnp.cos(turn_angle)
    sine_value = jnp.sin(turn_angle)
    return (
        real_part * cosine - imag_part * sine_value,
        imag_part * cosine + real_part * sine_value,
    )


def rotate_pair(field, turn_angle):
    real_part, imag_part = rotate(field[0], field[1], turn_angle)
    return jnp.stack([real_part, imag_part])


def filter_spectrum(residues, decay_rates, frequency, length_all):
    rates = jnp.transpose(decay_rates)[:, None, None, :]
    gains = jnp.transpose(residues)[:, None, None, :]
    phase_angle = frequency.astype(jnp.float32) * (2.0 * math.pi / length_all)
    half_sine = jnp.sin(0.5 * phase_angle)[None, :, :, None]
    full_sine = jnp.sin(phase_angle)[None, :, :, None]
    parity = (1 - 2 * (frequency % 2)).astype(jnp.float32)[None, :, :, None]
    retain = jnp.exp(-rates)
    shortfall = -jnp.expm1(-rates)
    weight = gains * jnp.sqrt(shortfall * (1.0 + retain))
    tail_factor = 1.0 - parity * jnp.exp(-rates * float(length_all // 2))
    denom_real = shortfall + 2.0 * retain * half_sine * half_sine
    denom_imag = retain * full_sine
    scale_factor = weight * tail_factor / (denom_real * denom_real + denom_imag * denom_imag)
    spec_real = jnp.sum(scale_factor * denom_real, axis=0)
    spec_imag = -jnp.sum(scale_factor * denom_imag, axis=0)
    return (spec_real, spec_imag)


def transform_rows(table, data):
    return jnp.einsum("kj,ejc->ekc", table, data, precision=HIGHEST)


def per_device(
    conv_input, residues, decay_rates, skip_gain, query_rows, key_rows, value_rows, norm_gain
):
    ctx_count = lax.axis_size("ctx")
    ctx_bits = ctx_count.bit_length() - 1
    position = lax.axis_index("ctx")
    row_count, chan_count = conv_input.shape
    length_all = 2 * ctx_count * row_count
    signal = conv_input.astype(jnp.float32)
    wave_index = jnp.arange(row_count, dtype=jnp.int32)
    two_index = jnp.arange(2, dtype=jnp.int32)
    start_angle = position.astype(jnp.float32) * (math.pi / ctx_count)
    zero_part = jnp.zeros_like(signal)
    field = jnp.stack(
        [
            jnp.stack([signal, signal * jnp.cos(start_angle)]),
            jnp.stack([zero_part, -signal * jnp.sin(start_angle)]),
        ]
    )
    for bit_index in range(ctx_bits - 1, -1, -1):
        half_span = 1 << bit_index
        partner = partner_2(field.astype(jnp.bfloat16), "ctx", bit_index).astype(field.dtype)
        upper_half = position >> bit_index & 1
        turn_angle = (position % half_span).astype(jnp.float32) * (-math.pi / half_span)
        field = jnp.where(
            upper_half == 1, rotate_pair(partner - field, turn_angle), field + partner
        )
    reversed_index = jnp.zeros((), jnp.int32)
    for bit_index in range(ctx_bits):
        reversed_index = reversed_index + (position >> bit_index & 1) * (
            1 << ctx_bits - 1 - bit_index
        )
    pair_freq = 2 * reversed_index + two_index
    turn_angle = (pair_freq[:, None] * wave_index[None, :] % length_all).astype(jnp.float32) * (
        -2.0 * math.pi / length_all
    )
    field = rotate_pair(field, turn_angle[:, :, None])
    rows_real = field[0]
    rows_imag = field[1]
    table_angle = (wave_index[:, None] * wave_index[None, :] % row_count).astype(jnp.float32) * (
        2.0 * math.pi / row_count
    )
    table_cos = jnp.cos(table_angle)
    table_sin = jnp.sin(table_angle)
    spec_real = transform_rows(table_cos, rows_real) + transform_rows(table_sin, rows_imag)
    spec_imag = transform_rows(table_cos, rows_imag) - transform_rows(table_sin, rows_real)
    frequency = pair_freq[:, None] + 2 * ctx_count * wave_index[None, :]
    filter_real, filter_imag = filter_spectrum(residues, decay_rates, frequency, length_all)
    product_real = spec_real * filter_real - spec_imag * filter_imag
    product_imag = spec_real * filter_imag + spec_imag * filter_real
    inverse_real = transform_rows(table_cos, product_real) - transform_rows(table_sin, product_imag)
    inverse_imag = transform_rows(table_cos, product_imag) + transform_rows(table_sin, product_real)
    turn_angle = (pair_freq[:, None] * wave_index[None, :] % length_all).astype(jnp.float32) * (
        2.0 * math.pi / length_all
    )
    inverse_real, inverse_imag = rotate(inverse_real, inverse_imag, turn_angle[:, :, None])
    field = jnp.stack([inverse_real, inverse_imag])
    for bit_index in range(ctx_bits):
        half_span = 1 << bit_index
        partner = partner_2(field.astype(jnp.bfloat16), "ctx", bit_index).astype(field.dtype)
        upper_half = position >> bit_index & 1
        turn_angle = (position % half_span).astype(jnp.float32) * (math.pi / half_span)
        field = jnp.where(
            upper_half == 1,
            partner - rotate_pair(field, turn_angle),
            field + rotate_pair(partner, turn_angle),
        )
    convolved = (
        field[0, 0] + jnp.cos(start_angle) * field[0, 1] - jnp.sin(start_angle) * field[1, 1]
    ) / length_all
    conv_out = (convolved + skip_gain[None, :] * signal).astype(jnp.bfloat16)
    gated = (value_rows.astype(jnp.float32) * conv_out.astype(jnp.float32)).astype(jnp.bfloat16)
    heads_here = query_rows.shape[1] // HD
    stacked = jnp.stack([key_rows, gated])
    previous = shifted(stacked, "ctx", 1)
    key_window = jnp.concatenate([previous[0], key_rows], axis=0).reshape(
        2 * row_count, heads_here, HD
    )
    value_window = jnp.concatenate([previous[1], gated], axis=0).reshape(
        2 * row_count, heads_here, HD
    )
    query_heads = query_rows.reshape(row_count, heads_here, HD)
    scores = jnp.einsum(
        "qhd,khd->hqk", query_heads, key_window, preferred_element_type=jnp.float32
    ) * HD ** (-0.5)
    query_place = jnp.arange(row_count, dtype=jnp.int32)[:, None]
    key_place = jnp.arange(2 * row_count, dtype=jnp.int32)[None, :] - row_count
    allowed = (key_place <= query_place) & ((key_place >= 0) | (position > 0))
    scores = jnp.where(allowed[None], scores, -jnp.inf)
    row_max = jnp.max(scores, axis=-1, keepdims=True)
    weights = jnp.exp(scores - row_max)
    row_total = jnp.sum(weights, axis=-1)
    mixed_heads = jnp.einsum(
        "hqk,khd->qhd",
        weights.astype(jnp.bfloat16),
        value_window,
        preferred_element_type=jnp.float32,
    )
    mixed_heads = mixed_heads / jnp.transpose(row_total)[:, :, None]
    attention = mixed_heads.reshape(row_count, heads_here * HD).astype(jnp.bfloat16)
    attention_wide = attention.astype(jnp.float32)
    energy = lax.psum(jnp.sum(attention_wide * attention_wide, axis=1), "ch")
    mean_square = energy / WIDTH
    attended = (
        attention_wide * norm_gain[None, :] / jnp.sqrt(mean_square + 1e-06)[:, None]
    ).astype(jnp.bfloat16)
    return (conv_out, attended)


def solution(mesh):
    return jax.shard_map(
        per_device,
        mesh=mesh,
        in_specs=(
            P("ctx", "ch"),
            P("ch", None),
            P("ch", None),
            P("ch"),
            P("ctx", "ch"),
            P("ctx", "ch"),
            P("ctx", "ch"),
            P("ch"),
        ),
        out_specs=(P("ctx", "ch"), P("ctx", "ch")),
        check_vma=False,
    )
```

profile of v0, /device:TPU:17, one launch (start us, length us, event | category | flops | bytes accessed | tf_op | source)
XLA Modules:
  0.0 565.2 jit_solution(9666510309292717080)
XLA Ops:
  0.8 1.3 copy.28
  2.7 1.9 fusion.14
  4.8 89.7 %collective-permute-done = bf16[2,2,128,2048]{2,3,1,0:T(8,128)(2,1)} collective-permute-done((bf16[2,2,128,2048]{2,3,1,0:T(8,128)(2,1)}, bf16[2,2,128,2048]{2,3,1,0:T(8,128)(2,1)}, u32[]{:S(2)}, u32[]{:S(2)}) %collective-permute-start) | collective-permute-done | bytes 2097184 | tf_op jit(solution)/shard_map/ppermute | solution.py:18
  94.5 2.6 convert_subtract_fusion.3
  98.7 4.2 fusion.126
  102.9 5.0 collective-permute-start.1
  108.1 45.6 %collective-permute-done.1 = bf16[2,2,128,2048]{2,3,1,0:T(8,128)(2,1)S(1)} collective-permute-done((bf16[2,2,128,2048]{2,3,1,0:T(8,128)(2,1)}, bf16[2,2,128,2048]{2,3,1,0:T(8,128)(2,1)S(1)}, u32[]{:S(2)}, u32[]{:S(2)}) %collective-permute-start.1) | collective-permute-done | bytes 2097184 | tf_op jit(solution)/shard_map/ppermute | solution.py:18
  153.7 2.5 convert_subtract_fusion.2
  156.7 1.7 copy-done.2
  158.4 3.4 fusion.124
  163.7 44.5 %collective-permute-done.2 = bf16[2,2,128,2048]{2,3,1,0:T(8,128)(2,1)S(1)} collective-permute-done((bf16[2,2,128,2048]{2,3,1,0:T(8,128)(2,1)}, bf16[2,2,128,2048]{2,3,1,0:T(8,128)(2,1)S(1)}, u32[]{:S(2)}, u32[]{:S(2)}) %collective-permute-start.2) | collective-permute-done | bytes 2097184 | tf_op jit(solution)/shard_map/ppermute | solution.py:18
  208.1 2.5 convert_subtract_fusion.1
  211.1 1.7 copy-done.1
  212.9 3.4 fusion.122
  217.5 21.2 %fusion.2 = (f32[2,128,2048]{2,1,0:T(8,128)}, f32[2,128,2048]{2,1,0:T(8,128)}) fusion(f32[2,128]{1,0:T(2,128)S(1)} %get-tuple-element.65, f32[16,2048]{1,0:T(8,128)S(1)} %get-tuple-element.58, f32[2,128]{1,0:T(2,128)S(1)} %get-tuple-element.66, f32[16,2048]{1,0:T(8,128)S(1)} %get-tuple-element.56, f32[16,2048]{1,0:T(8,128)S(1)} %get-tuple-element.59, ...), kind=kLoop, calls=%fused_computation.4 | loop fusion | flops 124780544 | bytes 4852736 | tf_op jit(solution)/shard_map/reduce_sum | solution.py:56
  238.7 1.9 copy.29
  240.6 3.1 copy.30
  243.7 18.0 %collective-permute-done.3 = bf16[2,2,128,2048]{2,3,1,0:T(8,128)(2,1)} collective-permute-done((bf16[2,2,128,2048]{2,3,1,0:T(8,128)(2,1)}, bf16[2,2,128,2048]{2,3,1,0:T(8,128)(2,1)}, u32[]{:S(2)}, u32[]{:S(2)}) %collective-permute-start.3) | collective-permute-done | bytes 2097184 | tf_op jit(solution)/shard_map/ppermute | solution.py:18
  261.8 3.2 convert_subtract_fusion
  265.3 1.9 copy-done.3
  267.2 2.1 fusion.6
  269.3 2.1 fusion.42
  271.3 2.1 fusion.43
  273.4 2.1 fusion.13
  275.5 2.4 multiply_subtract_fusion.8
  277.9 2.3 fusion.52
  280.2 2.1 fusion.54
  282.3 2.1 convolution_add_fusion
  284.5 2.6 fusion.17
  287.5 1.3 collective-permute-start.4
  289.0 42.8 %collective-permute-done.4 = bf16[2,2,128,2048]{2,3,1,0:T(8,128)(2,1)S(1)} collective-permute-done((bf16[2,2,128,2048]{2,3,1,0:T(8,128)(2,1)S(1)}, bf16[2,2,128,2048]{2,3,1,0:T(8,128)(2,1)S(1)}, u32[]{:S(2)}, u32[]{:S(2)}) %collective-permute-start.4) | collective-permute-done | bytes 2097184 | tf_op jit(solution)/shard_map/ppermute | solution.py:18
  332.4 3.0 fusion.120
  336.8 2.7 multiply_subtract_fusion.5
  339.4 39.5 %collective-permute-done.5 = bf16[2,2,128,2048]{2,3,1,0:T(8,128)(2,1)S(1)} collective-permute-done((bf16[2,2,128,2048]{2,3,1,0:T(8,128)(2,1)}, bf16[2,2,128,2048]{2,3,1,0:T(8,128)(2,1)S(1)}, u32[]{:S(2)}, u32[]{:S(2)}) %collective-permute-start.5) | collective-permute-done | bytes 2097184 | tf_op jit(solution)/shard_map/ppermute | solution.py:18
  379.7 1.7 copy-done.4
  381.4 3.1 fusion.118
  384.7 2.7 multiply_subtract_fusion.3
  387.3 39.8 %collective-permute-done.6 = bf16[2,2,128,2048]{2,3,1,0:T(8,128)(2,1)S(1)} collective-permute-done((bf16[2,2,128,2048]{2,3,1,0:T(8,128)(2,1)}, bf16[2,2,128,2048]{2,3,1,0:T(8,128)(2,1)S(1)}, u32[]{:S(2)}, u32[]{:S(2)}) %collective-permute-start.6) | collective-permute-done | bytes 2097184 | tf_op jit(solution)/shard_map/ppermute | solution.py:18
  427.9 1.7 copy-done.5
  429.6 3.3 fusion.116
  433.1 2.0 copy.33
  435.2 2.0 copy.32
  437.2 2.7 multiply_subtract_fusion.1
  439.9 83.2 %collective-permute-done.7 = bf16[2,2,128,2048]{2,3,1,0:T(8,128)(2,1)S(1)} collective-permute-done((bf16[2,2,128,2048]{2,3,1,0:T(8,128)(2,1)}, bf16[2,2,128,2048]{2,3,1,0:T(8,128)(2,1)S(1)}, u32[]{:S(2)}, u32[]{:S(2)}) %collective-permute-start.7) | collective-permute-done | bytes 2097184 | tf_op jit(solution)/shard_map/ppermute | solution.py:18
  523.8 1.7 copy-done.6
  528.7 3.1 collective-permute-start.8
  534.0 22.8 %collective-permute-done.8 = bf16[2,128,2048]{1,2,0:T(8,128)(2,1)S(1)} collective-permute-done((bf16[2,128,2048]{1,2,0:T(8,128)(2,1)}, bf16[2,128,2048]{1,2,0:T(8,128)(2,1)S(1)}, u32[]{:S(2)}, u32[]{:S(2)}) %collective-permute-start.8) | collective-permute-done | bytes 1048608 | tf_op jit(solution)/shard_map/ppermute | solution.py:24
  560.4 3.5 psum.7
  (75 shorter events, 20.5 us)
Async XLA Ops:
  0.6 557.3 %copy-start = (bf16[128,2048]{1,0:T(8,128)(2,1)S(1)}, bf16[128,2048]{1,0:T(8,128)(2,1)}, u32[]{:S(2)}) copy-start(bf16[128,2048]{1,0:T(8,128)(2,1)} %param.12) | copy-start | bytes 1572868
  2.7 2.0 copy-start.7
  4.7 89.9 %collective-permute-start = (bf16[2,2,128,2048]{2,3,1,0:T(8,128)(2,1)}, bf16[2,2,128,2048]{2,3,1,0:T(8,128)(2,1)}, u32[]{:S(2)}, u32[]{:S(2)}) collective-permute-start(bf16[2,2,128,2048]{2,3,1,0:T(8,128)(2,1)} %fusion.14), channel_id=1, source_target_pairs={{0,16},{2,18},{4,20},{6,22},{8,24},{10,26},{12,28},{14,30},{16,0},... | collective-permute-start | bytes 6291464 | tf_op jit(solution)/shard_map/ppermute | solution.py:18
  97.1 1.6 copy-start.8
  102.9 50.8 %collective-permute-start.1 = (bf16[2,2,128,2048]{2,3,1,0:T(8,128)(2,1)}, bf16[2,2,128,2048]{2,3,1,0:T(8,128)(2,1)S(1)}, u32[]{:S(2)}, u32[]{:S(2)}) collective-permute-start(bf16[2,2,128,2048]{2,3,1,0:T(8,128)(2,1)} %get-tuple-element.25), channel_id=1, source_target_pairs={{0,8},{2,10},{4,12},{6,14},{8,0},{10,2},{12,4},{14,6},{16,24},{18,... | collective-permute-start | bytes 6291464 | tf_op jit(solution)/shard_map/ppermute | solution.py:18
  156.2 2.2 copy-start.2
  158.4 5.1 copy-start.14
  158.4 5.1 copy-start.15
  161.8 46.3 %collective-permute-start.2 = (bf16[2,2,128,2048]{2,3,1,0:T(8,128)(2,1)}, bf16[2,2,128,2048]{2,3,1,0:T(8,128)(2,1)S(1)}, u32[]{:S(2)}, u32[]{:S(2)}) collective-permute-start(bf16[2,2,128,2048]{2,3,1,0:T(8,128)(2,1)} %get-tuple-element.23), channel_id=1, source_target_pairs={{0,4},{2,6},{4,0},{6,2},{8,12},{10,14},{12,8},{14,10},{16,20},{18,... | collective-permute-start | bytes 6291464 | tf_op jit(solution)/shard_map/ppermute | solution.py:18
  210.7 2.2 copy-start.1
  216.3 45.5 %collective-permute-start.3 = (bf16[2,2,128,2048]{2,3,1,0:T(8,128)(2,1)}, bf16[2,2,128,2048]{2,3,1,0:T(8,128)(2,1)}, u32[]{:S(2)}, u32[]{:S(2)}) collective-permute-start(bf16[2,2,128,2048]{2,3,1,0:T(8,128)(2,1)} %get-tuple-element.21), channel_id=1, source_target_pairs={{0,2},{2,0},{4,6},{6,4},{8,10},{10,8},{12,14},{14,12},{16,18},{18,... | collective-permute-start | bytes 6291464 | tf_op jit(solution)/shard_map/ppermute | solution.py:18
  265.0 2.2 copy-start.3
  273.4 2.1 copy-start.9
  287.5 44.3 %collective-permute-start.4 = (bf16[2,2,128,2048]{2,3,1,0:T(8,128)(2,1)S(1)}, bf16[2,2,128,2048]{2,3,1,0:T(8,128)(2,1)S(1)}, u32[]{:S(2)}, u32[]{:S(2)}) collective-permute-start(bf16[2,2,128,2048]{2,3,1,0:T(8,128)(2,1)S(1)} %fusion.11), channel_id=1, source_target_pairs={{0,2},{2,0},{4,6},{6,4},{8,10},{10,8},{12,14},{14,12},{16,18},{18,... | collective-permute-start | bytes 6291464 | tf_op jit(solution)/shard_map/ppermute | solution.py:18
  335.4 43.5 %collective-permute-start.5 = (bf16[2,2,128,2048]{2,3,1,0:T(8,128)(2,1)}, bf16[2,2,128,2048]{2,3,1,0:T(8,128)(2,1)S(1)}, u32[]{:S(2)}, u32[]{:S(2)}) collective-permute-start(bf16[2,2,128,2048]{2,3,1,0:T(8,128)(2,1)} %get-tuple-element.16), channel_id=1, source_target_pairs={{0,4},{2,6},{4,0},{6,2},{8,12},{10,14},{12,8},{14,10},{16,20},{18,... | collective-permute-start | bytes 6291464 | tf_op jit(solution)/shard_map/ppermute | solution.py:18
  379.2 2.2 copy-start.4
  384.5 42.6 %collective-permute-start.6 = (bf16[2,2,128,2048]{2,3,1,0:T(8,128)(2,1)}, bf16[2,2,128,2048]{2,3,1,0:T(8,128)(2,1)S(1)}, u32[]{:S(2)}, u32[]{:S(2)}) collective-permute-start(bf16[2,2,128,2048]{2,3,1,0:T(8,128)(2,1)} %get-tuple-element.14), channel_id=1, source_target_pairs={{0,8},{2,10},{4,12},{6,14},{8,0},{10,2},{12,4},{14,6},{16,24},{18,... | collective-permute-start | bytes 6291464 | tf_op jit(solution)/shard_map/ppermute | solution.py:18
  427.4 2.2 copy-start.5
  432.9 90.1 %collective-permute-start.7 = (bf16[2,2,128,2048]{2,3,1,0:T(8,128)(2,1)}, bf16[2,2,128,2048]{2,3,1,0:T(8,128)(2,1)S(1)}, u32[]{:S(2)}, u32[]{:S(2)}) collective-permute-start(bf16[2,2,128,2048]{2,3,1,0:T(8,128)(2,1)} %get-tuple-element.12), channel_id=1, source_target_pairs={{0,16},{2,18},{4,20},{6,22},{8,24},{10,26},{12,28},{14,30},{16,0},... | collective-permute-start | bytes 6291464 | tf_op jit(solution)/shard_map/ppermute | solution.py:18
  523.4 2.2 copy-start.6
  525.5 1.0 copy-start.11
  525.6 1.0 copy-start.16
  526.6 1.0 copy-start.10
  528.7 28.1 %collective-permute-start.8 = (bf16[2,128,2048]{1,2,0:T(8,128)(2,1)}, bf16[2,128,2048]{1,2,0:T(8,128)(2,1)S(1)}, u32[]{:S(2)}, u32[]{:S(2)}) collective-permute-start(bf16[2,128,2048]{1,2,0:T(8,128)(2,1)} %pad_maximum_fusion.2), channel_id=1, source_target_pairs={{0,2},{2,4},{4,6},{6,8},{8,10},{10,12},{12,14},{14,16},{16,18},{18... | collective-permute-start | bytes 3145736 | tf_op jit(solution)/shard_map/ppermute | solution.py:24
  534.0 24.0 %copy-start.12 = (bf16[128,16,128]{2,0,1:T(8,128)(2,1)S(1)}, bf16[128,16,128]{2,0,1:T(8,128)(2,1)}, u32[]{:S(2)}) copy-start(bf16[128,16,128]{2,0,1:T(8,128)(2,1)} %copy.36) | copy-start | bytes 1572868
  558.5 1.0 copy-start.13
  560.0 3.8 copy-start.17
where the time goes:
time: 575 us; the launch traced here: 565 us
  waiting for transfers between devices  426 us (74%)
  other arithmetic  73.9 us (13%)
  local copies, waits for them, and re-layouts  27.4 us (5%)
  matrix products  18.7 us (3%)
  starting transfers between devices  13.1 us (2%)
    ppermute x8, waiting for transfers between devices, partner_2(): return lax.ppermute(value, axis, pairs)  403 us
    ppermute x1, waiting for transfers between devices, shifted(): return lax.ppermute(block, axis, route)  22.8 us
    convert_element_type x8, other arithmetic, per_device(): field.astype(jnp.bfloat16)  22.7 us
    reduce_sum x1, other arithmetic, filter_spectrum(): spec_imag = -jnp.sum(scale_factor * denom_imag, axis=0)  21.2 us
    unnamed x40, local copies, waits for them, and re-layouts  19.9 us
    dot_general x8, matrix products, transform_rows(): return jnp.einsum('kj,ejc->ekc', table, data, precision=HIGHEST)  17.8 us
  transfers between devices with their start and end apart: 9, of which 9 were waited for; matrix products, arithmetic and copies ran while one was open for 7% of the time, Pallas kernels for 0%

commit v1 on v0

v1 whole, which is shorter than its diff:
```python
import functools
import math

import jax
import jax.numpy as jnp
import numpy as np
from jax import lax
from jax.experimental import pallas as pl
from jax.experimental.pallas import tpu as pltpu
from jax.sharding import PartitionSpec as P

HD = 128
LANES = 128
GROUP = 8
HEADS_PER_CHUNK = 4
MESH = pl.DeviceIdType.MESH


def scan_stages(count):
    stages = []
    stride = 1
    while stride < count:
        radix = 4 if count // stride >= 4 else 2
        stages.append((stride, radix))
        stride *= radix
    return stages


def split_bf16(value):
    high = value.astype(jnp.bfloat16)
    low = (value - high.astype(jnp.float32)).astype(jnp.bfloat16)
    return high, low


def dft_tables(rows):
    freq = 2 * np.arange(rows, dtype=np.int64)[:, None] + 1
    place = np.arange(rows, dtype=np.int64)[None, :]
    angle = (freq * place % (4 * rows)).astype(np.float64) * (math.pi / (2 * rows))
    forward = np.concatenate([np.cos(angle), -np.sin(angle)], axis=0)
    inverse = forward.T / rows
    parts = []
    for table in (forward, inverse):
        high = table.astype(jnp.bfloat16)
        low = (table - high.astype(np.float64)).astype(jnp.bfloat16)
        parts.append((high, low))
    (f_high, f_low), (i_high, i_low) = parts
    return (
        np.concatenate([f_high, f_low], axis=1),
        np.concatenate([f_high, f_high, f_low], axis=1),
        np.concatenate([i_high, i_high, i_low], axis=1),
    )


def kernel(
    ctx_count,
    ch_count,
    x_ref,
    rate_ref,
    res_ref,
    skip_ref,
    q_ref,
    k_ref,
    v_ref,
    gain_ref,
    fx_ref,
    fk_ref,
    inv_ref,
    conv_ref,
    out_ref,
    weight_s,
    taps_s,
    intra_s,
    state_s,
    enter_s,
    send_s,
    recv_s,
    gated_s,
    prev_k,
    prev_g,
    soft_s,
    own_s,
    norm_s,
    att_s,
    energy_s,
    energy_r,
    k_sem,
    g_send,
    g_recv,
    s_send,
    s_recv,
    e_send,
    e_recv,
):
    rows, chans = x_ref.shape
    modes = rate_ref.shape[0]
    tiles = chans // LANES
    groups = rows // GROUP
    heads = chans // HD
    chunks = heads // HEADS_PER_CHUNK
    chunk_cols = HEADS_PER_CHUNK * HD
    pos = lax.axis_index("ctx")
    core = lax.axis_index("ch")
    stages = scan_stages(ctx_count)

    offsets = {1}
    for stride, radix in stages:
        offsets |= {stride * m for m in range(1, radix)}
    offsets = sorted({o % ctx_count for o in offsets} | {-o % ctx_count for o in offsets})
    barrier = pltpu.get_barrier_semaphore()
    for o in offsets:
        pl.semaphore_signal(
            barrier, inc=1, device_id={"ctx": lax.rem(pos + o, ctx_count)}, device_id_type=MESH
        )
    for o in range(1, ch_count):
        pl.semaphore_signal(
            barrier, inc=1, device_id={"ch": lax.rem(core + o, ch_count)}, device_id_type=MESH
        )
    pl.semaphore_wait(barrier, len(offsets) + ch_count - 1)

    after = {"ctx": lax.rem(pos + 1, ctx_count)}
    has_after = pos + 1 < ctx_count
    has_before = pos > 0

    def key_copy():
        return pltpu.make_async_remote_copy(
            k_ref, prev_k, k_sem.at[0], k_sem.at[1], device_id=after, device_id_type=MESH
        )

    def gated_copy(c):
        part = pl.ds(c * chunk_cols, chunk_cols)
        return pltpu.make_async_remote_copy(
            gated_s.at[:, part],
            prev_g.at[:, part],
            g_send.at[c],
            g_recv.at[c],
            device_id=after,
            device_id_type=MESH,
        )

    def state_copy(level, slot, offset):
        return pltpu.make_async_remote_copy(
            send_s.at[level],
            recv_s.at[slot],
            s_send.at[slot],
            s_recv.at[slot],
            device_id={"ctx": lax.rem(pos + offset, ctx_count)},
            device_id_type=MESH,
        )

    @pl.when(has_after)
    def _():
        key_copy().start()

    @pl.when(jnp.logical_not(has_before))
    def _():
        prev_k[...] = jnp.zeros_like(prev_k)
        prev_g[...] = jnp.zeros_like(prev_g)

    u_place = lax.broadcasted_iota(jnp.int32, (1, GROUP, LANES), 1).astype(jnp.float32)

    def state_tile(j, carry):
        cols = pl.ds(pl.multiple_of(j * LANES, LANES), LANES)
        rate = rate_ref[:, cols]
        shrink = jnp.exp(-rate)
        weight_s[:, cols] = res_ref[:, cols] * jnp.sqrt((1.0 - shrink) * (1.0 + shrink))
        rate3 = rate[:, None, :]
        step = jnp.broadcast_to(jnp.exp(-GROUP * rate)[:, None, :], (modes, GROUP, LANES))
        x = x_ref[:, cols].astype(jnp.float32)
        total = jnp.broadcast_to(x[None, 0:GROUP], (modes, GROUP, LANES))
        for i in range(1, groups):
            total = total * step + x[None, i * GROUP : (i + 1) * GROUP]
        total = total * jnp.exp(-rate3 * (GROUP - 1.0 - u_place))
        state = jnp.sum(total, axis=1)
        state_s[:, cols] = state
        send_s[0, :, cols] = state.astype(jnp.bfloat16)
        return carry

    lax.fori_loop(0, tiles, state_tile, 0)

    def start_stage(level, base):
        stride, radix = stages[level]
        for m in range(1, radix):

            @pl.when(pos + m * stride < ctx_count)
            def _(m=m):
                state_copy(level, base + m - 1, m * stride).start()

            @pl.when(pos < m * stride)
            def _(m=m):
                recv_s[base + m - 1] = jnp.zeros(recv_s.shape[1:], recv_s.dtype)

    def wait_stage(level, base):
        stride, radix = stages[level]
        for m in range(1, radix):

            @pl.when(pos >= m * stride)
            def _(m=m):
                state_copy(level, base + m - 1, m * stride).wait_recv()

    def spread(cols, start):
        rate = rate_ref[:, cols]
        step = jnp.broadcast_to(jnp.exp(-GROUP * rate)[:, None, :], (modes, GROUP, LANES))
        term = start[:, None, :] * jnp.exp(-rate[:, None, :] * u_place)
        parts = []
        for i in range(groups):
            parts.append(jnp.sum(term, axis=0))
            if i + 1 < groups:
                term = term * step
        return jnp.concatenate(parts, axis=0)

    start_stage(0, 0)

    def taps_tile(j, carry):
        cols = pl.ds(pl.multiple_of(j * LANES, LANES), LANES)
        high, low = split_bf16(spread(cols, weight_s[:, cols]))
        taps_s[0:rows, cols] = high
        taps_s[rows : 2 * rows, cols] = low
        return carry

    lax.fori_loop(0, tiles, taps_tile, 0)

    wide = 2 * LANES

    def transform_tile(j, carry):
        cols = pl.ds(pl.multiple_of(j * wide, wide), wide)
        x = x_ref[:, cols]
        taps_high = taps_s[0:rows, cols]
        taps_low = taps_s[rows : 2 * rows, cols]
        spec = jnp.dot(
            fx_ref[...], jnp.concatenate([x, x], axis=0), preferred_element_type=jnp.float32
        )
        filt = jnp.dot(
            fk_ref[...],
            jnp.concatenate([taps_high, taps_low, taps_high], axis=0),
            preferred_element_type=jnp.float32,
        )
        s_re, s_im = spec[:rows], spec[rows:]
        f_re, f_im = filt[:rows], filt[rows:]
        product = jnp.concatenate([s_re * f_re - s_im * f_im, s_re * f_im + s_im * f_re], axis=0)
        high, low = split_bf16(product)
        intra_s[:, cols] = jnp.dot(
            inv_ref[...],
            jnp.concatenate([high, low, high], axis=0),
            preferred_element_type=jnp.float32,
        )
        return carry

    lax.fori_loop(0, chans // wide, transform_tile, 0)

    base = 0
    for level, (stride, radix) in enumerate(stages):
        wait_stage(level, base)
        last = level + 1 == len(stages)

        def combine_tile(j, carry, level=level, stride=stride, radix=radix, base=base, last=last):
            cols = pl.ds(pl.multiple_of(j * LANES, LANES), LANES)
            rate = rate_ref[:, cols] * float(rows)
            entered = jnp.zeros((modes, LANES), jnp.float32)
            total = state_s[:, cols]
            for m in range(1, radix):
                got = recv_s[base + m - 1, :, cols].astype(jnp.float32)
                entered = entered + jnp.exp(-rate * (m * stride - 1.0)) * got
                if not last:
                    total = total + jnp.exp(-rate * (1.0 * m * stride)) * got
            if level > 0:
                entered = entered + enter_s[:, cols]
            enter_s[:, cols] = entered
            if not last:
                state_s[:, cols] = total
                send_s[level + 1, :, cols] = total.astype(jnp.bfloat16)
            return carry

        lax.fori_loop(0, tiles, combine_tile, 0)
        base += radix - 1
        if not last:
            start_stage(level + 1, base)

    def gated_tile(j, carry):
        cols = pl.ds(pl.multiple_of(j * LANES, LANES), LANES)
        start = weight_s[:, cols] * enter_s[:, cols] * jnp.exp(-rate_ref[:, cols])
        x = x_ref[:, cols].astype(jnp.float32)
        conv = intra_s[:, cols] + spread(cols, start) + skip_ref[:, cols] * x
        conv = conv.astype(jnp.bfloat16)
        conv_ref[:, cols] = conv
        gated = v_ref[:, cols].astype(jnp.float32) * conv.astype(jnp.float32)
        gated_s[:, cols] = gated.astype(jnp.bfloat16)
        return carry

    for c in range(chunks):
        lax.fori_loop(c * HEADS_PER_CHUNK, (c + 1) * HEADS_PER_CHUNK, gated_tile, 0)

        @pl.when(has_after)
        def _(c=c):
            gated_copy(c).start()

    @pl.when(has_before)
    def _():
        key_copy().wait_recv()

    q_place = lax.broadcasted_iota(jnp.int32, (rows, rows), 0)
    k_place = lax.broadcasted_iota(jnp.int32, (rows, rows), 1)
    causal = k_place <= q_place
    before_bias = jnp.where(has_before, 0.0, -jnp.inf)
    contract = (((1,), (1,)), ((), ()))

    def weight_head(h, carry):
        cols = pl.ds(pl.multiple_of(h * HD, HD), HD)
        q = q_ref[:, cols]
        scale = HD ** (-0.5)
        old = lax.dot_general(q, prev_k[:, cols], contract, preferred_element_type=jnp.float32)
        new = lax.dot_general(q, k_ref[:, cols], contract, preferred_element_type=jnp.float32)
        old = old * scale + before_bias
        new = jnp.where(causal, new * scale, -jnp.inf)
        top = jnp.max(jnp.maximum(old, new), axis=1, keepdims=True)
        old = jnp.exp(old - top)
        new = jnp.exp(new - top)
        total = jnp.sum(old + new, axis=1, keepdims=True)
        soft_s[:, cols] = old.astype(jnp.bfloat16)
        own_s[:, cols] = jnp.dot(
            new.astype(jnp.bfloat16), gated_s[:, cols], preferred_element_type=jnp.float32
        )
        norm_s[:, cols] = jnp.broadcast_to(1.0 / total, (rows, HD))
        return carry

    lax.fori_loop(0, heads, weight_head, 0)

    energy_s[...] = jnp.zeros_like(energy_s)

    def mix_head(h, carry):
        cols = pl.ds(pl.multiple_of(h * HD, HD), HD)
        mixed = own_s[:, cols] + jnp.dot(
            soft_s[:, cols], prev_g[:, cols], preferred_element_type=jnp.float32
        )
        attention = (mixed * norm_s[:, cols]).astype(jnp.bfloat16)
        att_s[:, cols] = attention
        attention = attention.astype(jnp.float32)
        energy_s[...] += attention * attention
        return carry

    for c in range(chunks):

        @pl.when(has_before)
        def _(c=c):
            gated_copy(c).wait_recv()

        lax.fori_loop(c * HEADS_PER_CHUNK, (c + 1) * HEADS_PER_CHUNK, mix_head, 0)

    def energy_copy(o):
        return pltpu.make_async_remote_copy(
            energy_s,
            energy_r.at[o - 1],
            e_send.at[o - 1],
            e_recv.at[o - 1],
            device_id={"ch": lax.rem(core + o, ch_count)},
            device_id_type=MESH,
        )

    for o in range(1, ch_count):
        energy_copy(o).start()
    energy = energy_s[...]
    for o in range(1, ch_count):
        energy_copy(o).wait_recv()
        energy = energy + energy_r[o - 1]
    mean_square = jnp.sum(energy, axis=1, keepdims=True) / float(chans * ch_count)
    factor = jnp.broadcast_to(lax.rsqrt(mean_square + 1e-6), (rows, LANES))

    def norm_tile(j, carry):
        cols = pl.ds(pl.multiple_of(j * LANES, LANES), LANES)
        attention = att_s[:, cols].astype(jnp.float32)
        out_ref[:, cols] = (attention * gain_ref[:, cols] * factor).astype(jnp.bfloat16)
        return carry

    lax.fori_loop(0, tiles, norm_tile, 0)

    for o in range(1, ch_count):
        energy_copy(o).wait_send()

    @pl.when(has_after)
    def _():
        key_copy().wait_send()
        for c in range(chunks):
            gated_copy(c).wait_send()

    base = 0
    for level, (stride, radix) in enumerate(stages):
        for m in range(1, radix):

            @pl.when(pos + m * stride < ctx_count)
            def _(level=level, slot=base + m - 1, offset=m * stride):
                state_copy(level, slot, offset).wait_send()

        base += radix - 1


def per_device(
    conv_input, residues, decay_rates, skip_gain, query_rows, key_rows, value_rows, norm_gain
):
    ctx_count = lax.axis_size("ctx")
    ch_count = lax.axis_size("ch")
    rows, chans = conv_input.shape
    modes = residues.shape[1]
    chunks = chans // (HEADS_PER_CHUNK * HD)
    stages = scan_stages(ctx_count)
    slots = sum(radix - 1 for _, radix in stages)
    fx, fk, inv = (jnp.asarray(t) for t in dft_tables(rows))
    flat = jax.ShapeDtypeStruct((rows, chans), jnp.bfloat16)
    vmem = pl.BlockSpec(memory_space=pltpu.VMEM)
    dma = pltpu.SemaphoreType.DMA
    f32, b16 = jnp.float32, jnp.bfloat16
    return pl.pallas_call(
        functools.partial(kernel, ctx_count, ch_count),
        out_shape=(flat, flat),
        in_specs=[vmem] * 11,
        out_specs=(vmem, vmem),
        scratch_shapes=[
            pltpu.VMEM((modes, chans), f32),
            pltpu.VMEM((2 * rows, chans), b16),
            pltpu.VMEM((rows, chans), f32),
            pltpu.VMEM((modes, chans), f32),
            pltpu.VMEM((modes, chans), f32),
            pltpu.VMEM((len(stages), modes, chans), b16),
            pltpu.VMEM((slots, modes, chans), b16),
            pltpu.VMEM((rows, chans), b16),
            pltpu.VMEM((rows, chans), b16),
            pltpu.VMEM((rows, chans), b16),
            pltpu.VMEM((rows, chans), b16),
            pltpu.VMEM((rows, chans), f32),
            pltpu.VMEM((rows, chans), f32),
            pltpu.VMEM((rows, chans), b16),
            pltpu.VMEM((rows, LANES), f32),
            pltpu.VMEM((ch_count - 1, rows, LANES), f32),
            dma((2,)),
            dma((chunks,)),
            dma((chunks,)),
            dma((slots,)),
            dma((slots,)),
            dma((ch_count - 1,)),
            dma((ch_count - 1,)),
        ],
        compiler_params=pltpu.CompilerParams(
            collective_id=0, has_side_effects=True, vmem_limit_bytes=40 * 1024 * 1024
        ),
        cost_estimate=pl.CostEstimate(
            flops=4 * 10**9, bytes_accessed=4 * 10**6, transcendentals=10**6
        ),
    )(
        conv_input,
        jnp.transpose(decay_rates),
        jnp.transpose(residues),
        skip_gain[None, :],
        query_rows,
        key_rows,
        value_rows,
        norm_gain[None, :],
        fx,
        fk,
        inv,
    )


def solution(mesh):
    return jax.shard_map(
        per_device,
        mesh=mesh,
        in_specs=(
            P("ctx", "ch"),
            P("ch", None),
            P("ch", None),
            P("ch"),
            P("ctx", "ch"),
            P("ctx", "ch"),
            P("ctx", "ch"),
            P("ch"),
        ),
        out_specs=(P("ctx", "ch"), P("ctx", "ch")),
        check_vma=False,
    )
```

time: 575 us -> 55.4 us (0.10)
  the two profiles are of different devices: /device:TPU:17 before, /device:TPU:31 now
where the time goes in v1:
time: 55.4 us; the launch traced here: 54.9 us
  Pallas kernels  42.6 us (77%)
  local copies, waits for them, and re-layouts  11.7 us (21%)
  between operations  0.66 us (1%)
    pallas_call x1, Pallas kernels, per_device(): pl.pallas_call(functools.partial(kernel, ctx_count, ch_count), out_shape=...  42.6 us
    unnamed x24, local copies, waits for them, and re-layouts  11.7 us

profile of v1, /device:TPU:31, one launch (start us, length us, event | category | flops | bytes accessed | tf_op | source)
XLA Modules:
  0.0 54.9 jit_solution(1973215479055559368)
XLA Ops:
  0.6 0.0 copy-start
  0.6 1.0 %copy-done = bf16[128,2048]{1,0:T(8,128)(2,1)S(1)} copy-done((bf16[128,2048]{1,0:T(8,128)(2,1)S(1)}, bf16[128,2048]{1,0:T(8,128)(2,1)}, u32[]{:S(2)}) %copy-start) | copy-done | bytes 524312
  1.7 0.0 copy-start.1
  1.7 1.0 %copy-done.1 = bf16[128,2048]{1,0:T(8,128)(2,1)S(1)} copy-done((bf16[128,2048]{1,0:T(8,128)(2,1)S(1)}, bf16[128,2048]{1,0:T(8,128)(2,1)}, u32[]{:S(2)}) %copy-start.1) | copy-done | bytes 524312
  2.7 0.0 copy-start.2
  2.7 1.0 %copy-done.2 = bf16[128,2048]{1,0:T(8,128)(2,1)S(1)} copy-done((bf16[128,2048]{1,0:T(8,128)(2,1)S(1)}, bf16[128,2048]{1,0:T(8,128)(2,1)}, u32[]{:S(2)}) %copy-start.2) | copy-done | bytes 524312
  3.8 0.0 copy-start.3
  3.8 1.0 %copy-done.3 = bf16[128,2048]{1,0:T(8,128)(2,1)S(1)} copy-done((bf16[128,2048]{1,0:T(8,128)(2,1)S(1)}, bf16[128,2048]{1,0:T(8,128)(2,1)}, u32[]{:S(2)}) %copy-start.3) | copy-done | bytes 524312
  4.8 0.0 copy-start.4
  4.8 0.9 %copy-done.4 = f32[2048,16]{0,1:T(8,128)S(1)} copy-done((f32[2048,16]{0,1:T(8,128)S(1)}, f32[2048,16]{0,1:T(8,128)}, u32[]{:S(2)}) %copy-start.4) | copy-done | bytes 131096
  5.7 0.0 copy-start.5
  5.7 0.9 %copy-done.5 = f32[2048,16]{0,1:T(8,128)S(1)} copy-done((f32[2048,16]{0,1:T(8,128)S(1)}, f32[2048,16]{0,1:T(8,128)}, u32[]{:S(2)}) %copy-start.5) | copy-done | bytes 131096
  6.6 0.0 copy-start.6
  6.6 0.7 %copy-done.6 = f32[2048]{0:T(1024)S(1)} copy-done((f32[2048]{0:T(1024)S(1)}, f32[2048]{0:T(1024)}, u32[]{:S(2)}) %copy-start.6) | copy-done | bytes 8216
  7.3 0.0 copy-start.7
  7.3 0.7 %copy-done.7 = f32[2048]{0:T(1024)S(1)} copy-done((f32[2048]{0:T(1024)S(1)}, f32[2048]{0:T(1024)}, u32[]{:S(2)}) %copy-start.7) | copy-done | bytes 8216
  8.0 0.0 copy-start.8
  8.0 0.9 %copy-done.8 = bf16[128,768]{1,0:T(8,128)(2,1)S(1)} copy-done((bf16[128,768]{1,0:T(8,128)(2,1)S(1)}, bf16[128,768]{1,0:T(8,128)(2,1)}, u32[]{:S(2)}) %copy-start.8) | copy-done | bytes 196632
  8.9 0.0 copy-start.9
  8.9 0.9 %copy-done.9 = bf16[256,384]{1,0:T(8,128)(2,1)S(1)} copy-done((bf16[256,384]{1,0:T(8,128)(2,1)S(1)}, bf16[256,384]{1,0:T(8,128)(2,1)}, u32[]{:S(2)}) %copy-start.9) | copy-done | bytes 196632
  9.9 0.0 copy-start.10
  9.9 0.9 %copy-done.10 = bf16[256,256]{1,0:T(8,128)(2,1)S(1)} copy-done((bf16[256,256]{1,0:T(8,128)(2,1)S(1)}, bf16[256,256]{1,0:T(8,128)(2,1)}, u32[]{:S(2)}) %copy-start.10) | copy-done | bytes 131096
  10.8 42.6 %shard_map.122 = (bf16[128,2048]{1,0:T(8,128)(2,1)S(1)}, bf16[128,2048]{1,0:T(8,128)(2,1)S(1)}) custom-call(bf16[128,2048]{1,0:T(8,128)(2,1)S(1)} %copy-done, f32[16,2048]{1,0:T(8,128)S(1)} %bitcast.4, f32[16,2048]{1,0:T(8,128)S(1)} %bitcast.5, f32[1,2048]{1,0:T(1,128)S(1)} %bitcast.6, bf16[128,2048]{1,0:T(8,128)(2,1)S(1)} %copy-done.1, ...), custom_call_target="tpu_custom_call" | custom-call | flops 4000000000 | bytes 4000000 | tf_op jit(solution)/shard_map/pallas_call | solution.py:410
  53.3 0.8 %copy.15 = bf16[128,2048]{1,0:T(8,128)(2,1)} copy(bf16[128,2048]{1,0:T(8,128)(2,1)S(1)} %get-tuple-element.4) | data formatting | bytes 1048576
  54.1 0.8 %copy.16 = bf16[128,2048]{1,0:T(8,128)(2,1)} copy(bf16[128,2048]{1,0:T(8,128)(2,1)S(1)} %get-tuple-element.5) | data formatting | bytes 1048576
Async XLA Ops:
  0.6 1.0 %copy-start = (bf16[128,2048]{1,0:T(8,128)(2,1)S(1)}, bf16[128,2048]{1,0:T(8,128)(2,1)}, u32[]{:S(2)}) copy-start(bf16[128,2048]{1,0:T(8,128)(2,1)} %x_ref.1) | copy-start | bytes 1572868
  1.7 1.0 %copy-start.1 = (bf16[128,2048]{1,0:T(8,128)(2,1)S(1)}, bf16[128,2048]{1,0:T(8,128)(2,1)}, u32[]{:S(2)}) copy-start(bf16[128,2048]{1,0:T(8,128)(2,1)} %q_ref.1) | copy-start | bytes 1572868
  2.7 1.0 %copy-start.2 = (bf16[128,2048]{1,0:T(8,128)(2,1)S(1)}, bf16[128,2048]{1,0:T(8,128)(2,1)}, u32[]{:S(2)}) copy-start(bf16[128,2048]{1,0:T(8,128)(2,1)} %k_ref.1) | copy-start | bytes 1572868
  3.8 1.0 %copy-start.3 = (bf16[128,2048]{1,0:T(8,128)(2,1)S(1)}, bf16[128,2048]{1,0:T(8,128)(2,1)}, u32[]{:S(2)}) copy-start(bf16[128,2048]{1,0:T(8,128)(2,1)} %v_ref.1) | copy-start | bytes 1572868
  4.8 0.9 %copy-start.4 = (f32[2048,16]{0,1:T(8,128)S(1)}, f32[2048,16]{0,1:T(8,128)}, u32[]{:S(2)}) copy-start(f32[2048,16]{0,1:T(8,128)} %param.13) | copy-start | bytes 393220
  5.7 0.9 %copy-start.5 = (f32[2048,16]{0,1:T(8,128)S(1)}, f32[2048,16]{0,1:T(8,128)}, u32[]{:S(2)}) copy-start(f32[2048,16]{0,1:T(8,128)} %param.12) | copy-start | bytes 393220
  6.6 0.7 %copy-start.6 = (f32[2048]{0:T(1024)S(1)}, f32[2048]{0:T(1024)}, u32[]{:S(2)}) copy-start(f32[2048]{0:T(1024)} %param.14) | copy-start | bytes 24580
  7.3 0.7 %copy-start.7 = (f32[2048]{0:T(1024)S(1)}, f32[2048]{0:T(1024)}, u32[]{:S(2)}) copy-start(f32[2048]{0:T(1024)} %param.18) | copy-start | bytes 24580
  8.0 0.9 %copy-start.8 = (bf16[128,768]{1,0:T(8,128)(2,1)S(1)}, bf16[128,768]{1,0:T(8,128)(2,1)}, u32[]{:S(2)}) copy-start(bf16[128,768]{1,0:T(8,128)(2,1)} %constant.8.clone.inv_ref) | copy-start | bytes 589828
  8.9 0.9 %copy-start.9 = (bf16[256,384]{1,0:T(8,128)(2,1)S(1)}, bf16[256,384]{1,0:T(8,128)(2,1)}, u32[]{:S(2)}) copy-start(bf16[256,384]{1,0:T(8,128)(2,1)} %constant.7.clone.fk_ref) | copy-start | bytes 589828
  9.9 0.9 %copy-start.10 = (bf16[256,256]{1,0:T(8,128)(2,1)S(1)}, bf16[256,256]{1,0:T(8,128)(2,1)}, u32[]{:S(2)}) copy-start(bf16[256,256]{1,0:T(8,128)(2,1)} %constant.6.clone.fx_ref) | copy-start | bytes 393220

commit v2 on v1

--- a/solution.py
+++ b/solution.py
@@ -38,22 +38,24 @@
     angle = (freq * place % (4 * rows)).astype(np.float64) * (math.pi / (2 * rows))
     forward = np.concatenate([np.cos(angle), -np.sin(angle)], axis=0)
     inverse = forward.T / rows
-    parts = []
-    for table in (forward, inverse):
-        high = table.astype(jnp.bfloat16)
-        low = (table - high.astype(np.float64)).astype(jnp.bfloat16)
-        parts.append((high, low))
-    (f_high, f_low), (i_high, i_low) = parts
-    return (
-        np.concatenate([f_high, f_low], axis=1),
-        np.concatenate([f_high, f_high, f_low], axis=1),
-        np.concatenate([i_high, i_high, i_low], axis=1),
-    )
+    return forward.astype(np.float32), inverse.astype(np.float32)
 
 
 def kernel(
     ctx_count,
     ch_count,
+    x_hbm,
+    rate_hbm,
+    res_hbm,
+    skip_hbm,
+    q_hbm,
+    k_hbm,
+    v_hbm,
+    gain_hbm,
+    fwd_hbm,
+    inv_hbm,
+    conv_ref,
+    out_ref,
     x_ref,
     rate_ref,
     res_ref,
@@ -62,11 +64,12 @@
     k_ref,
     v_ref,
     gain_ref,
-    fx_ref,
-    fk_ref,
+    fwd_ref,
     inv_ref,
-    conv_ref,
-    out_ref,
+    fx_s,
+    fk_s,
+    inv_s,
+    load_sem,
     weight_s,
     taps_s,
     intra_s,
@@ -83,7 +86,8 @@
     att_s,
     energy_s,
     energy_r,
-    k_sem,
+    k_send,
+    k_recv,
     g_send,
     g_recv,
     s_send,
@@ -91,6 +95,24 @@
     e_send,
     e_recv,
 ):
+    loads = {}
+    for i, (name, source, target) in enumerate(
+        (
+            ("rate", rate_hbm, rate_ref),
+            ("x", x_hbm, x_ref),
+            ("res", res_hbm, res_ref),
+            ("fwd", fwd_hbm, fwd_ref),
+            ("inv", inv_hbm, inv_ref),
+            ("skip", skip_hbm, skip_ref),
+            ("v", v_hbm, v_ref),
+            ("k", k_hbm, k_ref),
+            ("q", q_hbm, q_ref),
+            ("gain", gain_hbm, gain_ref),
+        )
+    ):
+        loads[name] = pltpu.make_async_copy(source, target, load_sem.at[i])
+        loads[name].start()
+
     rows, chans = x_ref.shape
     modes = rate_ref.shape[0]
     tiles = chans // LANES
@@ -120,10 +142,17 @@
     after = {"ctx": lax.rem(pos + 1, ctx_count)}
     has_after = pos + 1 < ctx_count
     has_before = pos > 0
-
-    def key_copy():
+    early = chunks // 2
+
+    def key_copy(c):
+        part = pl.ds(c * chunk_cols, chunk_cols)
         return pltpu.make_async_remote_copy(
-            k_ref, prev_k, k_sem.at[0], k_sem.at[1], device_id=after, device_id_type=MESH
+            k_hbm.at[:, part],
+            prev_k.at[:, part],
+            k_send.at[c],
+            k_recv.at[c],
+            device_id=after,
+            device_id_type=MESH,
         )
 
     def gated_copy(c):
@@ -149,7 +178,8 @@
 
     @pl.when(has_after)
     def _():
-        key_copy().start()
+        for c in range(early):
+            key_copy(c).start()
 
     @pl.when(jnp.logical_not(has_before))
     def _():
@@ -175,6 +205,9 @@
         send_s[0, :, cols] = state.astype(jnp.bfloat16)
         return carry
 
+    loads["rate"].wait()
+    loads["res"].wait()
+    loads["x"].wait()
     lax.fori_loop(0, tiles, state_tile, 0)
 
     def start_stage(level, base):
@@ -227,10 +260,10 @@
         taps_high = taps_s[0:rows, cols]
         taps_low = taps_s[rows : 2 * rows, cols]
         spec = jnp.dot(
-            fx_ref[...], jnp.concatenate([x, x], axis=0), preferred_element_type=jnp.float32
+            fx_s[...], jnp.concatenate([x, x], axis=0), preferred_element_type=jnp.float32
         )
         filt = jnp.dot(
-            fk_ref[...],
+            fk_s[...],
             jnp.concatenate([taps_high, taps_low, taps_high], axis=0),
             preferred_element_type=jnp.float32,
         )
@@ -239,13 +272,12 @@
         product = jnp.concatenate([s_re * f_re - s_im * f_im, s_re * f_im + s_im * f_re], axis=0)
         high, low = split_bf16(product)
         intra_s[:, cols] = jnp.dot(
-            inv_ref[...],
+            inv_s[...],
             jnp.concatenate([high, low, high], axis=0),
             preferred_element_type=jnp.float32,
         )
         return carry
 
-    lax.fori_loop(0, chans // wide, transform_tile, 0)
 
     base = 0
     for level, (stride, radix) in enumerate(stages):
@@ -274,6 +306,23 @@
         base += radix - 1
         if not last:
             start_stage(level + 1, base)
+        if level == 0:
+
+            @pl.when(has_after)
+            def _():
+                for c in range(early, chunks):
+                    key_copy(c).start()
+
+            loads["fwd"].wait()
+            loads["inv"].wait()
+            high, low = split_bf16(fwd_ref[...])
+            fx_s[...] = jnp.concatenate([high, low], axis=1)
+            fk_s[...] = jnp.concatenate([high, high, low], axis=1)
+            high, low = split_bf16(inv_ref[...])
+            inv_s[...] = jnp.concatenate([high, high, low], axis=1)
+            lax.fori_loop(0, chans // wide, transform_tile, 0)
+            loads["skip"].wait()
+            loads["v"].wait()
 
     def gated_tile(j, carry):
         cols = pl.ds(pl.multiple_of(j * LANES, LANES), LANES)
@@ -293,9 +342,14 @@
         def _(c=c):
             gated_copy(c).start()
 
+    loads["q"].wait()
+    loads["k"].wait()
+    loads["gain"].wait()
+
     @pl.when(has_before)
     def _():
-        key_copy().wait_recv()
+        for c in range(chunks):
+            key_copy(c).wait_recv()
 
     q_place = lax.broadcasted_iota(jnp.int32, (rows, rows), 0)
     k_place = lax.broadcasted_iota(jnp.int32, (rows, rows), 1)
@@ -377,8 +431,8 @@
 
     @pl.when(has_after)
     def _():
-        key_copy().wait_send()
         for c in range(chunks):
+            key_copy(c).wait_send()
             gated_copy(c).wait_send()
 
     base = 0
@@ -402,17 +456,32 @@
     chunks = chans // (HEADS_PER_CHUNK * HD)
     stages = scan_stages(ctx_count)
     slots = sum(radix - 1 for _, radix in stages)
-    fx, fk, inv = (jnp.asarray(t) for t in dft_tables(rows))
+    fwd, inv = (jnp.asarray(t) for t in dft_tables(rows))
     flat = jax.ShapeDtypeStruct((rows, chans), jnp.bfloat16)
     vmem = pl.BlockSpec(memory_space=pltpu.VMEM)
+    hbm = pl.BlockSpec(memory_space=pltpu.HBM)
     dma = pltpu.SemaphoreType.DMA
     f32, b16 = jnp.float32, jnp.bfloat16
     return pl.pallas_call(
         functools.partial(kernel, ctx_count, ch_count),
         out_shape=(flat, flat),
-        in_specs=[vmem] * 11,
+        in_specs=[hbm] * 10,
         out_specs=(vmem, vmem),
         scratch_shapes=[
+            pltpu.VMEM((rows, chans), b16),
+            pltpu.VMEM((modes, chans), f32),
+            pltpu.VMEM((modes, chans), f32),
+            pltpu.VMEM((1, chans), f32),
+            pltpu.VMEM((rows, chans), b16),
+            pltpu.VMEM((rows, chans), b16),
+            pltpu.VMEM((rows, chans), b16),
+            pltpu.VMEM((1, chans), f32),
+            pltpu.VMEM(fwd.shape, f32),
+            pltpu.VMEM(inv.shape, f32),
+            pltpu.VMEM((2 * rows, 2 * rows), b16),
+            pltpu.VMEM((2 * rows, 3 * rows), b16),
+            pltpu.VMEM((rows, 6 * rows), b16),
+            dma((10,)),
             pltpu.VMEM((modes, chans), f32),
             pltpu.VMEM((2 * rows, chans), b16),
             pltpu.VMEM((rows, chans), f32),
@@ -429,7 +498,8 @@
             pltpu.VMEM((rows, chans), b16),
             pltpu.VMEM((rows, LANES), f32),
             pltpu.VMEM((ch_count - 1, rows, LANES), f32),
-            dma((2,)),
+            dma((chunks,)),
+            dma((chunks,)),
             dma((chunks,)),
             dma((chunks,)),
             dma((slots,)),
@@ -438,7 +508,7 @@
             dma((ch_count - 1,)),
         ],
         compiler_params=pltpu.CompilerParams(
-            collective_id=0, has_side_effects=True, vmem_limit_bytes=40 * 1024 * 1024
+            collective_id=0, has_side_effects=True, vmem_limit_bytes=63 * 1024 * 1024
         ),
         cost_estimate=pl.CostEstimate(
             flops=4 * 10**9, bytes_accessed=4 * 10**6, transcendentals=10**6
@@ -452,8 +522,7 @@
         key_rows,
         value_rows,
         norm_gain[None, :],
-        fx,
-        fk,
+        fwd,
         inv,
     )
 

time: 55.4 us -> 46.5 us (0.84)
  the two profiles are of different devices: /device:TPU:31 before, /device:TPU:17 now
where the time goes in v2:
time: 46.5 us; the launch traced here: 46.3 us
  Pallas kernels  42.9 us (92%)
  local copies, waits for them, and re-layouts  2.74 us (6%)
  between operations  0.65 us (1%)
    pallas_call x1, Pallas kernels, per_device(): pl.pallas_call(functools.partial(kernel, ctx_count, ch_count), out_shape=...  42.9 us
    unnamed x4, local copies, waits for them, and re-layouts  2.74 us

profile of v2, /device:TPU:17, one launch (start us, length us, event | category | flops | bytes accessed | tf_op | source)
XLA Modules:
  0.0 46.3 jit_solution(17942234720647811487)
XLA Ops:
  0.6 42.9 %shard_map.113 = (bf16[128,2048]{1,0:T(8,128)(2,1)}, bf16[128,2048]{1,0:T(8,128)(2,1)}) custom-call(bf16[128,2048]{1,0:T(8,128)(2,1)} %x_hbm.1, f32[16,2048]{1,0:T(8,128)} %bitcast.4, f32[16,2048]{1,0:T(8,128)} %bitcast.5, f32[1,2048]{1,0:T(1,128)} %bitcast.6, bf16[128,2048]{1,0:T(8,128)(2,1)} %q_hbm.1, bf16[128,2048]{1,0:T(8,128)(2,1)} %k_hbm.1, ...), custom_call_target="tpu_custom_call" | custom-call | flops 4000000000 | bytes 4000000 | tf_op jit(solution)/shard_map/pallas_call | solution.py:465
  43.6 0.0 copy-start
  43.6 1.9 %copy.14 = bf16[128,2048]{1,0:T(8,128)(2,1)} copy(bf16[128,2048]{1,0:T(8,128)(2,1)} %get-tuple-element.4) | data formatting | bytes 1048576
  45.5 0.0 copy-done
  45.5 0.8 %copy.15 = bf16[128,2048]{1,0:T(8,128)(2,1)} copy(bf16[128,2048]{1,0:T(8,128)(2,1)S(1)} %copy-done) | data formatting | bytes 1048576
Async XLA Ops:
  43.6 2.0 %copy-start = (bf16[128,2048]{1,0:T(8,128)(2,1)S(1)}, bf16[128,2048]{1,0:T(8,128)(2,1)}, u32[]{:S(2)}) copy-start(bf16[128,2048]{1,0:T(8,128)(2,1)} %get-tuple-element.5) | copy-start | bytes 1572868

commit v3 on v2

--- a/solution.py
+++ b/solution.py
@@ -254,7 +254,7 @@
 
     wide = 2 * LANES
 
-    def transform_tile(j, carry):
+    def transform_part(j):
         cols = pl.ds(pl.multiple_of(j * wide, wide), wide)
         x = x_ref[:, cols]
         taps_high = taps_s[0:rows, cols]
@@ -271,13 +271,17 @@
         f_re, f_im = filt[:rows], filt[rows:]
         product = jnp.concatenate([s_re * f_re - s_im * f_im, s_re * f_im + s_im * f_re], axis=0)
         high, low = split_bf16(product)
-        intra_s[:, cols] = jnp.dot(
+        return cols, jnp.dot(
             inv_s[...],
             jnp.concatenate([high, low, high], axis=0),
             preferred_element_type=jnp.float32,
         )
-        return carry
-
+
+
+    def transform_tile(j, carry):
+        for cols, value in [transform_part(2 * j), transform_part(2 * j + 1)]:
+            intra_s[:, cols] = value
+        return carry
 
     base = 0
     for level, (stride, radix) in enumerate(stages):
@@ -320,7 +324,7 @@
             fk_s[...] = jnp.concatenate([high, high, low], axis=1)
             high, low = split_bf16(inv_ref[...])
             inv_s[...] = jnp.concatenate([high, high, low], axis=1)
-            lax.fori_loop(0, chans // wide, transform_tile, 0)
+            lax.fori_loop(0, chans // (2 * wide), transform_tile, 0)
             loads["skip"].wait()
             loads["v"].wait()
 
@@ -357,38 +361,56 @@
     before_bias = jnp.where(has_before, 0.0, -jnp.inf)
     contract = (((1,), (1,)), ((), ()))
 
-    def weight_head(h, carry):
-        cols = pl.ds(pl.multiple_of(h * HD, HD), HD)
-        q = q_ref[:, cols]
+    def weight_chunk(c, carry):
+        start = c * chunk_cols
+        parts = [
+            pl.ds(start + h * HD if isinstance(start, int) else pl.multiple_of(start + h * HD, HD), HD)
+            for h in range(HEADS_PER_CHUNK)
+        ]
         scale = HD ** (-0.5)
-        old = lax.dot_general(q, prev_k[:, cols], contract, preferred_element_type=jnp.float32)
-        new = lax.dot_general(q, k_ref[:, cols], contract, preferred_element_type=jnp.float32)
-        old = old * scale + before_bias
-        new = jnp.where(causal, new * scale, -jnp.inf)
-        top = jnp.max(jnp.maximum(old, new), axis=1, keepdims=True)
-        old = jnp.exp(old - top)
-        new = jnp.exp(new - top)
-        total = jnp.sum(old + new, axis=1, keepdims=True)
-        soft_s[:, cols] = old.astype(jnp.bfloat16)
-        own_s[:, cols] = jnp.dot(
-            new.astype(jnp.bfloat16), gated_s[:, cols], preferred_element_type=jnp.float32
-        )
-        norm_s[:, cols] = jnp.broadcast_to(1.0 / total, (rows, HD))
-        return carry
-
-    lax.fori_loop(0, heads, weight_head, 0)
+        scores = []
+        for cols in parts:
+            q = q_ref[:, cols]
+            old = lax.dot_general(q, prev_k[:, cols], contract, preferred_element_type=jnp.float32)
+            new = lax.dot_general(q, k_ref[:, cols], contract, preferred_element_type=jnp.float32)
+            scores.append((old * scale + before_bias, jnp.where(causal, new * scale, -jnp.inf)))
+        tops = [jnp.max(jnp.maximum(old, new), axis=1, keepdims=True) for old, new in scores]
+        weights = [
+            (jnp.exp(old - top), jnp.exp(new - top)) for (old, new), top in zip(scores, tops)
+        ]
+        totals = [jnp.sum(old + new, axis=1, keepdims=True) for old, new in weights]
+        mixes = [
+            jnp.dot(new.astype(jnp.bfloat16), gated_s[:, cols], preferred_element_type=jnp.float32)
+            for (_, new), cols in zip(weights, parts)
+        ]
+        for cols, (old, _), total, mix in zip(parts, weights, totals, mixes):
+            soft_s[:, cols] = old.astype(jnp.bfloat16)
+            own_s[:, cols] = mix
+            norm_s[:, cols] = jnp.broadcast_to(1.0 / total, (rows, HD))
+        return carry
+
+    lax.fori_loop(0, chunks, weight_chunk, 0)
 
     energy_s[...] = jnp.zeros_like(energy_s)
 
-    def mix_head(h, carry):
-        cols = pl.ds(pl.multiple_of(h * HD, HD), HD)
-        mixed = own_s[:, cols] + jnp.dot(
-            soft_s[:, cols], prev_g[:, cols], preferred_element_type=jnp.float32
-        )
-        attention = (mixed * norm_s[:, cols]).astype(jnp.bfloat16)
-        att_s[:, cols] = attention
-        attention = attention.astype(jnp.float32)
-        energy_s[...] += attention * attention
+    def mix_chunk(c, carry):
+        start = c * chunk_cols
+        parts = [
+            pl.ds(start + h * HD if isinstance(start, int) else pl.multiple_of(start + h * HD, HD), HD)
+            for h in range(HEADS_PER_CHUNK)
+        ]
+        mixes = [
+            own_s[:, cols]
+            + jnp.dot(soft_s[:, cols], prev_g[:, cols], preferred_element_type=jnp.float32)
+            for cols in parts
+        ]
+        mixes = [(m * norm_s[:, cols]).astype(jnp.bfloat16) for m, cols in zip(mixes, parts)]
+        total = energy_s[...]
+        for cols, attention in zip(parts, mixes):
+            att_s[:, cols] = attention
+            attention = attention.astype(jnp.float32)
+            total = total + attention * attention
+        energy_s[...] = total
         return carry
 
     for c in range(chunks):
@@ -397,7 +419,7 @@
         def _(c=c):
             gated_copy(c).wait_recv()
 
-        lax.fori_loop(c * HEADS_PER_CHUNK, (c + 1) * HEADS_PER_CHUNK, mix_head, 0)
+        mix_chunk(c, 0)
 
     def energy_copy(o):
         return pltpu.make_async_remote_copy(

time: 46.5 us -> 46 us (0.989)
  no operation moved by 1% of the time
where the time goes in v3:
time: 46 us; the launch traced here: 45.9 us
  Pallas kernels  42.5 us (92%)
  local copies, waits for them, and re-layouts  2.74 us (6%)
  between operations  0.65 us (1%)
    pallas_call x1, Pallas kernels, per_device(): pl.pallas_call(functools.partial(kernel, ctx_count, ch_count), out_shape=...  42.5 us
    unnamed x4, local copies, waits for them, and re-layouts  2.74 us

profile of v3, /device:TPU:17, one launch (start us, length us, event | category | flops | bytes accessed | tf_op | source)
XLA Modules:
  0.0 45.9 jit_solution(2408934377028458321)
XLA Ops:
  0.6 42.5 %shard_map.113 = (bf16[128,2048]{1,0:T(8,128)(2,1)}, bf16[128,2048]{1,0:T(8,128)(2,1)}) custom-call(bf16[128,2048]{1,0:T(8,128)(2,1)} %x_hbm.1, f32[16,2048]{1,0:T(8,128)} %bitcast.4, f32[16,2048]{1,0:T(8,128)} %bitcast.5, f32[1,2048]{1,0:T(1,128)} %bitcast.6, bf16[128,2048]{1,0:T(8,128)(2,1)} %q_hbm.1, bf16[128,2048]{1,0:T(8,128)(2,1)} %k_hbm.1, ...), custom_call_target="tpu_custom_call" | custom-call | flops 4000000000 | bytes 4000000 | tf_op jit(solution)/shard_map/pallas_call | solution.py:487
  43.1 0.0 copy-start
  43.2 1.9 %copy.14 = bf16[128,2048]{1,0:T(8,128)(2,1)} copy(bf16[128,2048]{1,0:T(8,128)(2,1)} %get-tuple-element.4) | data formatting | bytes 1048576
  45.1 0.0 copy-done
  45.1 0.8 %copy.15 = bf16[128,2048]{1,0:T(8,128)(2,1)} copy(bf16[128,2048]{1,0:T(8,128)(2,1)S(1)} %copy-done) | data formatting | bytes 1048576
Async XLA Ops:
  43.1 2.0 %copy-start = (bf16[128,2048]{1,0:T(8,128)(2,1)S(1)}, bf16[128,2048]{1,0:T(8,128)(2,1)}, u32[]{:S(2)}) copy-start(bf16[128,2048]{1,0:T(8,128)(2,1)} %get-tuple-element.5) | copy-start | bytes 1572868

commit v4 on v3

--- a/solution.py
+++ b/solution.py
@@ -142,7 +142,7 @@
     after = {"ctx": lax.rem(pos + 1, ctx_count)}
     has_after = pos + 1 < ctx_count
     has_before = pos > 0
-    early = chunks // 2
+    early = chunks
 
     def key_copy(c):
         part = pl.ds(c * chunk_cols, chunk_cols)

time: 46 us -> 47.1 us (1.024)
  the two profiles are of different devices: /device:TPU:17 before, /device:TPU:31 now
where the time goes in v4:
time: 47.1 us; the launch traced here: 47 us
  Pallas kernels  43.6 us (93%)
  local copies, waits for them, and re-layouts  2.74 us (6%)
  between operations  0.65 us (1%)
    pallas_call x1, Pallas kernels, per_device(): pl.pallas_call(functools.partial(kernel, ctx_count, ch_count), out_shape=...  43.6 us
    unnamed x4, local copies, waits for them, and re-layouts  2.74 us

profile of v4, /device:TPU:31, one launch (start us, length us, event | category | flops | bytes accessed | tf_op | source)
XLA Modules:
  0.0 47.0 jit_solution(17500959210824635113)
XLA Ops:
  0.6 43.6 %shard_map.113 = (bf16[128,2048]{1,0:T(8,128)(2,1)}, bf16[128,2048]{1,0:T(8,128)(2,1)}) custom-call(bf16[128,2048]{1,0:T(8,128)(2,1)} %x_hbm.1, f32[16,2048]{1,0:T(8,128)} %bitcast.4, f32[16,2048]{1,0:T(8,128)} %bitcast.5, f32[1,2048]{1,0:T(1,128)} %bitcast.6, bf16[128,2048]{1,0:T(8,128)(2,1)} %q_hbm.1, bf16[128,2048]{1,0:T(8,128)(2,1)} %k_hbm.1, ...), custom_call_target="tpu_custom_call" | custom-call | flops 4000000000 | bytes 4000000 | tf_op jit(solution)/shard_map/pallas_call | solution.py:487
  44.2 0.0 copy-start
  44.2 1.9 %copy.14 = bf16[128,2048]{1,0:T(8,128)(2,1)} copy(bf16[128,2048]{1,0:T(8,128)(2,1)} %get-tuple-element.4) | data formatting | bytes 1048576
  46.2 0.0 copy-done
  46.2 0.8 %copy.15 = bf16[128,2048]{1,0:T(8,128)(2,1)} copy(bf16[128,2048]{1,0:T(8,128)(2,1)S(1)} %copy-done) | data formatting | bytes 1048576
Async XLA Ops:
  44.2 2.0 %copy-start = (bf16[128,2048]{1,0:T(8,128)(2,1)S(1)}, bf16[128,2048]{1,0:T(8,128)(2,1)}, u32[]{:S(2)}) copy-start(bf16[128,2048]{1,0:T(8,128)(2,1)} %get-tuple-element.5) | copy-start | bytes 1572868

commit v5 on v4

--- a/solution.py
+++ b/solution.py
@@ -142,7 +142,7 @@
     after = {"ctx": lax.rem(pos + 1, ctx_count)}
     has_after = pos + 1 < ctx_count
     has_before = pos > 0
-    early = chunks
+    early = chunks // 4
 
     def key_copy(c):
         part = pl.ds(c * chunk_cols, chunk_cols)

time: 47.1 us -> 45.3 us (0.962)
  the two profiles are of different devices: /device:TPU:31 before, /device:TPU:17 now
where the time goes in v5:
time: 45.3 us; the launch traced here: 45.2 us
  Pallas kernels  41.8 us (92%)
  local copies, waits for them, and re-layouts  2.74 us (6%)
  between operations  0.65 us (1%)
    pallas_call x1, Pallas kernels, per_device(): pl.pallas_call(functools.partial(kernel, ctx_count, ch_count), out_shape=...  41.8 us
    unnamed x4, local copies, waits for them, and re-layouts  2.74 us

profile of v5, /device:TPU:17, one launch (start us, length us, event | category | flops | bytes accessed | tf_op | source)
XLA Modules:
  0.0 45.2 jit_solution(780063820334498301)
XLA Ops:
  0.6 41.8 %shard_map.113 = (bf16[128,2048]{1,0:T(8,128)(2,1)}, bf16[128,2048]{1,0:T(8,128)(2,1)}) custom-call(bf16[128,2048]{1,0:T(8,128)(2,1)} %x_hbm.1, f32[16,2048]{1,0:T(8,128)} %bitcast.4, f32[16,2048]{1,0:T(8,128)} %bitcast.5, f32[1,2048]{1,0:T(1,128)} %bitcast.6, bf16[128,2048]{1,0:T(8,128)(2,1)} %q_hbm.1, bf16[128,2048]{1,0:T(8,128)(2,1)} %k_hbm.1, ...), custom_call_target="tpu_custom_call" | custom-call | flops 4000000000 | bytes 4000000 | tf_op jit(solution)/shard_map/pallas_call | solution.py:487
  42.4 0.0 copy-start
  42.5 1.9 %copy.14 = bf16[128,2048]{1,0:T(8,128)(2,1)} copy(bf16[128,2048]{1,0:T(8,128)(2,1)} %get-tuple-element.4) | data formatting | bytes 1048576
  44.4 0.0 copy-done
  44.4 0.8 %copy.15 = bf16[128,2048]{1,0:T(8,128)(2,1)} copy(bf16[128,2048]{1,0:T(8,128)(2,1)S(1)} %copy-done) | data formatting | bytes 1048576
Async XLA Ops:
  42.4 2.0 %copy-start = (bf16[128,2048]{1,0:T(8,128)(2,1)S(1)}, bf16[128,2048]{1,0:T(8,128)(2,1)}, u32[]{:S(2)}) copy-start(bf16[128,2048]{1,0:T(8,128)(2,1)} %get-tuple-element.5) | copy-start | bytes 1572868

commit v6 on v5

--- a/solution.py
+++ b/solution.py
@@ -142,7 +142,7 @@
     after = {"ctx": lax.rem(pos + 1, ctx_count)}
     has_after = pos + 1 < ctx_count
     has_before = pos > 0
-    early = chunks // 4
+    early = 0
 
     def key_copy(c):
         part = pl.ds(c * chunk_cols, chunk_cols)

time: 45.3 us -> 46.9 us (1.035)
  Pallas kernels: 41.8 us -> 42.9 us
    pallas_call x1, Pallas kernels: 41.8 us -> 42.9 us  [per_device(): pl.pallas_call(functools.partial(kernel, ctx_count, ch_count), out_shape=...]
where the time goes in v6:
time: 46.9 us; the launch traced here: 46.3 us
  Pallas kernels  42.9 us (91%)
  local copies, waits for them, and re-layouts  2.74 us (6%)
  between operations  0.65 us (1%)
    pallas_call x1, Pallas kernels, per_device(): pl.pallas_call(functools.partial(kernel, ctx_count, ch_count), out_shape=...  42.9 us
    unnamed x4, local copies, waits for them, and re-layouts  2.74 us

profile of v6, /device:TPU:17, one launch (start us, length us, event | category | flops | bytes accessed | tf_op | source)
XLA Modules:
  0.0 46.3 jit_solution(16806046336357355260)
XLA Ops:
  0.6 42.9 %shard_map.113 = (bf16[128,2048]{1,0:T(8,128)(2,1)}, bf16[128,2048]{1,0:T(8,128)(2,1)}) custom-call(bf16[128,2048]{1,0:T(8,128)(2,1)} %x_hbm.1, f32[16,2048]{1,0:T(8,128)} %bitcast.4, f32[16,2048]{1,0:T(8,128)} %bitcast.5, f32[1,2048]{1,0:T(1,128)} %bitcast.6, bf16[128,2048]{1,0:T(8,128)(2,1)} %q_hbm.1, bf16[128,2048]{1,0:T(8,128)(2,1)} %k_hbm.1, ...), custom_call_target="tpu_custom_call" | custom-call | flops 4000000000 | bytes 4000000 | tf_op jit(solution)/shard_map/pallas_call | solution.py:487
  43.6 0.0 copy-start
  43.6 1.9 %copy.14 = bf16[128,2048]{1,0:T(8,128)(2,1)} copy(bf16[128,2048]{1,0:T(8,128)(2,1)} %get-tuple-element.4) | data formatting | bytes 1048576
  45.5 0.0 copy-done
  45.5 0.8 %copy.15 = bf16[128,2048]{1,0:T(8,128)(2,1)} copy(bf16[128,2048]{1,0:T(8,128)(2,1)S(1)} %copy-done) | data formatting | bytes 1048576
Async XLA Ops:
  43.6 2.0 %copy-start = (bf16[128,2048]{1,0:T(8,128)(2,1)S(1)}, bf16[128,2048]{1,0:T(8,128)(2,1)}, u32[]{:S(2)}) copy-start(bf16[128,2048]{1,0:T(8,128)(2,1)} %get-tuple-element.5) | copy-start | bytes 1572868
